TPU v7x, 512 devices: a whole 4x4x16 slice. The times are simulated.
512 devices in a mesh: view: 8 (over z_hi, y), seq: 64 (over z_lo, x, core).
Axes of the slice: x: 4, y: 4, z: 16 (z_hi: 2, z_lo: 8; z = z_hi * 8 + z_lo), core: 2. Of those that a mesh axis runs over, the one named last changes fastest.
Arguments:
- queries: bfloat16 [4, 8, 2048, 2048], P(None, 'view', 'seq'), may hold values from -6 to 6
- key_rows: bfloat16 [4, 8, 2048, 2048], P(None, 'view', 'seq'), may hold values from -6 to 6
- value_rows: bfloat16 [4, 8, 2048, 2048], P(None, 'view', 'seq'), may hold values from -6 to 6
- view_queries: bfloat16 [4, 8, 2048, 2048], P(None, 'view', 'seq'), may hold values from -6 to 6
Outputs:
- spatial: bfloat16 [4, 8, 2048, 2048], P(None, 'view', 'seq')
- joined: bfloat16 [4, 8, 2048, 2048], P(None, 'view', 'seq')
All inputs are finite; a program needn't handle non-finite values.
Results may differ from a plain program's by a relative error of at most 0.0064.
Values may be sent and summed in bfloat16 or wider, within the bound.
A program may use at most 64 MiB of HBM per device.

v0:
```python
import jax
import jax.numpy as jnp
from jax import lax
from jax.sharding import PartitionSpec as P

HEADS = 32


def split_heads(tokens):
    batch_size, single, local_len, model_width = tokens.shape
    shaped = tokens.reshape(batch_size, local_len, HEADS, model_width // HEADS)
    return shaped.transpose(1, 0, 2, 3).reshape(local_len, batch_size * HEADS, model_width // HEADS)


def merge_heads(pairs, batch_size):
    local_len, pair_count, head_width = pairs.shape
    shaped = pairs.reshape(local_len, batch_size, pair_count // batch_size, head_width)
    return shaped.transpose(1, 0, 2, 3).reshape(
        batch_size, 1, local_len, pair_count // batch_size * head_width
    )


def attend(query_pairs, key_pairs, value_pairs):
    length, pair_count, head_width = query_pairs.shape
    block_rows = min(512, length)
    score_scale = head_width ** (-0.5)

    def one_block(query_block):
        scores = (
            jnp.einsum("qpe,kpe->pqk", query_block, key_pairs, preferred_element_type=jnp.float32)
            * score_scale
        )
        scores = scores - jnp.max(scores, axis=-1, keepdims=True)
        expo = jnp.exp(scores)
        weights = (expo / jnp.sum(expo, axis=-1, keepdims=True)).astype(jnp.bfloat16)
        result = jnp.einsum(
            "pqk,kpe->qpe", weights, value_pairs, preferred_element_type=jnp.float32
        )
        return result.astype(jnp.bfloat16)

    blocks = query_pairs.reshape(length // block_rows, block_rows, pair_count, head_width)
    return lax.map(one_block, blocks).reshape(length, pair_count, head_width)


def view_weights(cross_query, key_part):
    batch_size, view_count, few_rows, model_width = cross_query.shape
    head_width = model_width // HEADS
    split_shape = (batch_size, view_count, few_rows, HEADS, head_width)
    score_scale = head_width ** (-0.5)
    scores = (
        jnp.einsum(
            "bvngd,bwngd->bngvw",
            cross_query.reshape(split_shape),
            key_part.reshape(split_shape),
            preferred_element_type=jnp.float32,
        )
        * score_scale
    )
    scores = scores - jnp.max(scores, axis=-1, keepdims=True)
    expo = jnp.exp(scores)
    return (expo / jnp.sum(expo, axis=-1, keepdims=True)).astype(jnp.bfloat16)


def apply_weights(weights, output_part):
    batch_size, view_count, few_rows, model_width = output_part.shape
    head_width = model_width // HEADS
    split_shape = (batch_size, view_count, few_rows, HEADS, head_width)
    result = jnp.einsum(
        "bngvw,bwngd->bvngd",
        weights,
        output_part.reshape(split_shape),
        preferred_element_type=jnp.float32,
    )
    return result.astype(jnp.bfloat16).reshape(batch_size, view_count, few_rows, model_width)


def local(queries, key_rows, value_rows, view_queries):
    batch_size = queries.shape[0]
    query_pairs, key_pairs, value_pairs = (
        lax.all_to_all(split_heads(queries), "seq", split_axis=1, concat_axis=0, tiled=True),
        lax.all_to_all(split_heads(key_rows), "seq", split_axis=1, concat_axis=0, tiled=True),
        lax.all_to_all(split_heads(value_rows), "seq", split_axis=1, concat_axis=0, tiled=True),
    )
    output_pairs = attend(query_pairs, key_pairs, value_pairs)
    returned = lax.all_to_all(output_pairs, "seq", split_axis=0, concat_axis=1, tiled=True)
    spatial = merge_heads(returned, batch_size)
    cross_query, key_views, output_views = (
        lax.all_to_all(view_queries, "view", split_axis=2, concat_axis=1, tiled=True),
        lax.all_to_all(key_rows, "view", split_axis=2, concat_axis=1, tiled=True),
        lax.all_to_all(spatial, "view", split_axis=2, concat_axis=1, tiled=True),
    )
    mixing = view_weights(cross_query, key_views)
    combined = apply_weights(mixing, output_views)
    joined = lax.all_to_all(combined, "view", split_axis=1, concat_axis=2, tiled=True)
    return (spatial, joined)


def solution(mesh):
    placed = (
        P(None, "view", "seq", None),
        P(None, "view", "seq", None),
        P(None, "view", "seq", None),
        P(None, "view", "seq", None),
    )
    return jax.shard_map(
        local,
        mesh=mesh,
        in_specs=placed,
        out_specs=(P(None, "view", "seq", None), P(None, "view", "seq", None)),
        check_vma=False,
    )
```

profile of v0, /device:TPU:32, one launch (start us, length us, event | category | flops | bytes accessed | tf_op | source)
XLA Modules:
  0.0 335.2 jit_solution(2345342563840960147)
XLA Ops:
  5.1 15.7 %all-to-all-start = ((bf16[64,2,2048]{2,1,0:T(2,128)(2,1)}), bf16[64,2,2048]{2,1,0:T(2,128)(2,1)S(1)}, u32[]{:S(2)}, u32[]{:S(2)}) async-start(bf16[64,2,2048]{2,1,0:T(2,128)(2,1)} %reshape.85), calls=%async_computation | async-start | bytes 1048576 | tf_op jit(solution)/shard_map/all_to_all | solution.py:80
  24.3 24.8 %all-to-all-done = bf16[64,2,2048]{2,1,0:T(2,128)(2,1)S(1)} async-done(((bf16[64,2,2048]{2,1,0:T(2,128)(2,1)}), bf16[64,2,2048]{2,1,0:T(2,128)(2,1)S(1)}, u32[]{:S(2)}, u32[]{:S(2)}) %all-to-all-start) | async-done | bytes 524320 | tf_op jit(solution)/shard_map/all_to_all | solution.py:80
  49.0 8.6 %all-to-all-start.1 = ((bf16[64,2,2048]{2,1,0:T(2,128)(2,1)}), bf16[64,2,2048]{2,1,0:T(2,128)(2,1)S(1)}, u32[]{:S(2)}, u32[]{:S(2)}) async-start(bf16[64,2,2048]{2,1,0:T(2,128)(2,1)} %reshape.87), calls=%async_computation.1 | async-start | bytes 1048576 | tf_op jit(solution)/shard_map/all_to_all | solution.py:81
  61.1 24.8 %all-to-all-done.1 = bf16[64,2,2048]{2,1,0:T(2,128)(2,1)S(1)} async-done(((bf16[64,2,2048]{2,1,0:T(2,128)(2,1)}), bf16[64,2,2048]{2,1,0:T(2,128)(2,1)S(1)}, u32[]{:S(2)}, u32[]{:S(2)}) %all-to-all-start.1) | async-done | bytes 524320 | tf_op jit(solution)/shard_map/all_to_all | solution.py:81
  85.8 8.8 %all-to-all-start.2 = ((bf16[64,2,2048]{2,1,0:T(2,128)(2,1)}), bf16[64,2,2048]{2,1,0:T(2,128)(2,1)}, u32[]{:S(2)}, u32[]{:S(2)}) async-start(bf16[64,2,2048]{2,1,0:T(2,128)(2,1)} %reshape.89), calls=%async_computation.2 | async-start | bytes 1048576 | tf_op jit(solution)/shard_map/all_to_all | solution.py:82
  99.7 23.0 %all-to-all-done.2 = bf16[64,2,2048]{2,1,0:T(2,128)(2,1)} async-done(((bf16[64,2,2048]{2,1,0:T(2,128)(2,1)}), bf16[64,2,2048]{2,1,0:T(2,128)(2,1)}, u32[]{:S(2)}, u32[]{:S(2)}) %all-to-all-start.2) | async-done | bytes 524320 | tf_op jit(solution)/shard_map/all_to_all | solution.py:82
  122.8 10.2 %all-to-all-start.5 = ((bf16[4,1,32,2048]{3,0,1,2:T(4,128)(2,1)}), bf16[4,1,32,2048]{3,0,1,2:T(4,128)(2,1)S(1)}, u32[]{:S(2)}, u32[]{:S(2)}) async-start(bf16[4,1,32,2048]{3,0,1,2:T(4,128)(2,1)} %copy.99), calls=%async_computation.5 | async-start | bytes 1048576 | tf_op jit(solution)/shard_map/all_to_all | solution.py:88
  135.7 49.4 %while.10 = (s32[]{:T(128)}, bf16[4,512,2,64]{1,3,2,0:T(8,128)(2,1)}, bf16[4,512,2,64]{1,3,2,0:T(8,128)(2,1)}, bf16[2048,2,64]{0,2,1:T(8,128)(2,1)}, bf16[2048,2,64]{0,2,1:T(8,128)(2,1)S(1)}, /*index=5*/s32[]{:T(128)}) while((s32[]{:T(128)}, bf16[4,512,2,64]{1,3,2,0:T(8,128)(2,1)}, bf16[4,512,2,64]{1,3,2,0:T(8,128)(2,1)}, ...), condition=%wide.region_3.4_spmd, body=%wide.region_0.3_spmd.sunk | while | flops 547424256 | bytes 18097220 | solution.py:42
  135.7 6.8 %fusion.70 = (f32[2,512]{1,0:T(2,128)S(1)}, f32[2,512,2048]{2,1,0:T(8,128)}) fusion(bf16[2048,2,64]{0,2,1:T(8,128)(2,1)} %get-tuple-element.120, bf16[4,512,2,64]{1,3,2,0:T(8,128)(2,1)} %get-tuple-element.119, s32[]{:T(128)} %get-tuple-element.111), kind=kOutput, calls=%fused_computation.33.clone.1 | convolution fusion | flops 274728960 | bytes 9048576 | tf_op jit(solution)/shard_map/while/body/eval_jaxpr/sub | solution.py:33
  142.6 5.5 %fusion.71 = bf16[4,512,2,64]{1,3,2,0:T(8,128)(2,1)} fusion(bf16[4,512,2,64]{1,3,2,0:T(8,128)(2,1)} %get-tuple-element.112, s32[]{:T(128)} %get-tuple-element.111, bf16[2048,2,64]{0,2,1:T(8,128)(2,1)S(1)} %get-tuple-element.121, f32[2,512,2048]{2,1,0:T(8,128)} %get-tuple-element.103, f32[2,512]{1,0:T(2,128)S(1)} %get-tuple-element.104), kind=kOutput, calls=%fused_computation.9.clone.1 | convolution fusion | flops 272695296 | bytes 9048576 | tf_op jit(solution)/shard_map/while/body/eval_jaxpr/pqk,kpe->qpe/dot_general | solution.py:36
  148.1 6.8 %fusion.70 = (f32[2,512]{1,0:T(2,128)S(1)}, f32[2,512,2048]{2,1,0:T(8,128)}) fusion(bf16[2048,2,64]{0,2,1:T(8,128)(2,1)} %get-tuple-element.120, bf16[4,512,2,64]{1,3,2,0:T(8,128)(2,1)} %get-tuple-element.119, s32[]{:T(128)} %get-tuple-element.111), kind=kOutput, calls=%fused_computation.33.clone.1 | convolution fusion | flops 274728960 | bytes 9048576 | tf_op jit(solution)/shard_map/while/body/eval_jaxpr/sub | solution.py:33
  154.9 5.5 %fusion.71 = bf16[4,512,2,64]{1,3,2,0:T(8,128)(2,1)} fusion(bf16[4,512,2,64]{1,3,2,0:T(8,128)(2,1)} %get-tuple-element.112, s32[]{:T(128)} %get-tuple-element.111, bf16[2048,2,64]{0,2,1:T(8,128)(2,1)S(1)} %get-tuple-element.121, f32[2,512,2048]{2,1,0:T(8,128)} %get-tuple-element.103, f32[2,512]{1,0:T(2,128)S(1)} %get-tuple-element.104), kind=kOutput, calls=%fused_computation.9.clone.1 | convolution fusion | flops 272695296 | bytes 9048576 | tf_op jit(solution)/shard_map/while/body/eval_jaxpr/pqk,kpe->qpe/dot_general | solution.py:36
  160.4 6.8 %fusion.70 = (f32[2,512]{1,0:T(2,128)S(1)}, f32[2,512,2048]{2,1,0:T(8,128)}) fusion(bf16[2048,2,64]{0,2,1:T(8,128)(2,1)} %get-tuple-element.120, bf16[4,512,2,64]{1,3,2,0:T(8,128)(2,1)} %get-tuple-element.119, s32[]{:T(128)} %get-tuple-element.111), kind=kOutput, calls=%fused_computation.33.clone.1 | convolution fusion | flops 274728960 | bytes 9048576 | tf_op jit(solution)/shard_map/while/body/eval_jaxpr/sub | solution.py:33
  167.2 5.5 %fusion.71 = bf16[4,512,2,64]{1,3,2,0:T(8,128)(2,1)} fusion(bf16[4,512,2,64]{1,3,2,0:T(8,128)(2,1)} %get-tuple-element.112, s32[]{:T(128)} %get-tuple-element.111, bf16[2048,2,64]{0,2,1:T(8,128)(2,1)S(1)} %get-tuple-element.121, f32[2,512,2048]{2,1,0:T(8,128)} %get-tuple-element.103, f32[2,512]{1,0:T(2,128)S(1)} %get-tuple-element.104), kind=kOutput, calls=%fused_computation.9.clone.1 | convolution fusion | flops 272695296 | bytes 9048576 | tf_op jit(solution)/shard_map/while/body/eval_jaxpr/pqk,kpe->qpe/dot_general | solution.py:36
  172.7 6.8 %fusion.70 = (f32[2,512]{1,0:T(2,128)S(1)}, f32[2,512,2048]{2,1,0:T(8,128)}) fusion(bf16[2048,2,64]{0,2,1:T(8,128)(2,1)} %get-tuple-element.120, bf16[4,512,2,64]{1,3,2,0:T(8,128)(2,1)} %get-tuple-element.119, s32[]{:T(128)} %get-tuple-element.111), kind=kOutput, calls=%fused_computation.33.clone.1 | convolution fusion | flops 274728960 | bytes 9048576 | tf_op jit(solution)/shard_map/while/body/eval_jaxpr/sub | solution.py:33
  179.6 5.5 %fusion.71 = bf16[4,512,2,64]{1,3,2,0:T(8,128)(2,1)} fusion(bf16[4,512,2,64]{1,3,2,0:T(8,128)(2,1)} %get-tuple-element.112, s32[]{:T(128)} %get-tuple-element.111, bf16[2048,2,64]{0,2,1:T(8,128)(2,1)S(1)} %get-tuple-element.121, f32[2,512,2048]{2,1,0:T(8,128)} %get-tuple-element.103, f32[2,512]{1,0:T(2,128)S(1)} %get-tuple-element.104), kind=kOutput, calls=%fused_computation.9.clone.1 | convolution fusion | flops 272695296 | bytes 9048576 | tf_op jit(solution)/shard_map/while/body/eval_jaxpr/pqk,kpe->qpe/dot_general | solution.py:36
  189.0 8.6 %all-to-all-start.3 = ((bf16[64,2,2048]{2,1,0:T(2,128)(2,1)}), bf16[64,2,2048]{2,1,0:T(2,128)(2,1)S(1)}, u32[]{:S(2)}, u32[]{:S(2)}) async-start(bf16[64,2,2048]{2,1,0:T(2,128)(2,1)} %reshape.91), calls=%async_computation.3 | async-start | bytes 1048576 | tf_op jit(solution)/shard_map/all_to_all | solution.py:85
  198.8 27.0 %all-to-all-done.3 = bf16[64,2,2048]{2,1,0:T(2,128)(2,1)S(1)} async-done(((bf16[64,2,2048]{2,1,0:T(2,128)(2,1)}), bf16[64,2,2048]{2,1,0:T(2,128)(2,1)S(1)}, u32[]{:S(2)}, u32[]{:S(2)}) %all-to-all-start.3) | async-done | bytes 524320 | tf_op jit(solution)/shard_map/all_to_all | solution.py:85
  225.8 14.4 %all-to-all-start.6 = ((bf16[4,1,32,2048]{3,0,1,2:T(4,128)(2,1)}), bf16[4,1,32,2048]{3,0,1,2:T(4,128)(2,1)S(1)}, u32[]{:S(2)}, u32[]{:S(2)}) async-start(bf16[4,1,32,2048]{3,0,1,2:T(4,128)(2,1)} %copy.101), calls=%async_computation.6 | async-start | bytes 1048576 | tf_op jit(solution)/shard_map/all_to_all | solution.py:89
  243.6 31.9 %all-to-all-done.6 = bf16[4,1,32,2048]{3,0,1,2:T(4,128)(2,1)S(1)} async-done(((bf16[4,1,32,2048]{3,0,1,2:T(4,128)(2,1)}), bf16[4,1,32,2048]{3,0,1,2:T(4,128)(2,1)S(1)}, u32[]{:S(2)}, u32[]{:S(2)}) %all-to-all-start.6) | async-done | bytes 524320 | tf_op jit(solution)/shard_map/all_to_all | solution.py:89
  275.5 3.5 %all-to-all-start.4 = ((bf16[4,1,32,2048]{3,0,1,2:T(4,128)(2,1)}), bf16[4,1,32,2048]{3,0,1,2:T(4,128)(2,1)S(1)}, u32[]{:S(2)}, u32[]{:S(2)}) async-start(bf16[4,1,32,2048]{3,0,1,2:T(4,128)(2,1)} %copy.97), calls=%async_computation.4 | async-start | bytes 1048576 | tf_op jit(solution)/shard_map/all_to_all | solution.py:90
  281.6 4.7 %fusion.54 = (f32[4,4,32,8]{3,2,1,0:T(8,128)S(1)}, f32[4,4,32,8,8]{3,4,2,1,0:T(8,128)}) fusion(bf16[4,8,4,32,64]{4,3,0,2,1:T(8,128)(2,1)} %reshape.83, bf16[4,8,4,32,64]{4,3,0,2,1:T(8,128)(2,1)S(1)} %reshape.82), kind=kOutput, calls=%fused_computation.34 | convolution fusion | flops 4292615 | bytes 1196032 | tf_op jit(solution)/shard_map/sub | solution.py:59
  286.3 13.0 %all-to-all-done.4 = bf16[4,1,32,2048]{3,0,1,2:T(4,128)(2,1)S(1)} async-done(((bf16[4,1,32,2048]{3,0,1,2:T(4,128)(2,1)}), bf16[4,1,32,2048]{3,0,1,2:T(4,128)(2,1)S(1)}, u32[]{:S(2)}, u32[]{:S(2)}) %all-to-all-start.4) | async-done | bytes 524320 | tf_op jit(solution)/shard_map/all_to_all | solution.py:90
  303.7 30.1 %all_to_all.105 = bf16[4,8,4,2048]{3,2,0,1:T(4,128)(2,1)S(1)} all-to-all(bf16[4,8,4,2048]{3,2,0,1:T(4,128)(2,1)S(1)} %reshape.84), channel_id=1, replica_groups=mesh['view'=8,'seq'=64] {'view'}, dimensions={1} | all-to-all | bytes 1048576 | tf_op jit(solution)/shard_map/all_to_all | solution.py:94
  (49 shorter events, 36.0 us)
Async XLA Ops:
  0.6 20.2 %copy-start = (bf16[4,1,32,2048]{3,2,1,0:T(8,128)(2,1)S(1)}, bf16[4,1,32,2048]{3,2,1,0:T(8,128)(2,1)}, u32[]{:S(2)}) copy-start(bf16[4,1,32,2048]{3,2,1,0:T(8,128)(2,1)} %param.7) | copy-start | bytes 1572868
  5.1 43.9 %all-to-all-start = ((bf16[64,2,2048]{2,1,0:T(2,128)(2,1)}), bf16[64,2,2048]{2,1,0:T(2,128)(2,1)S(1)}, u32[]{:S(2)}, u32[]{:S(2)}) async-start(bf16[64,2,2048]{2,1,0:T(2,128)(2,1)} %reshape.85), calls=%async_computation | async-start | bytes 1048576 | tf_op jit(solution)/shard_map/all_to_all | solution.py:80
  20.8 36.8 %copy-start.2 = (bf16[4,1,32,2048]{3,2,1,0:T(8,128)(2,1)S(1)}, bf16[4,1,32,2048]{3,2,1,0:T(8,128)(2,1)}, u32[]{:S(2)}) copy-start(bf16[4,1,32,2048]{3,2,1,0:T(8,128)(2,1)} %param.8) | copy-start | bytes 1572868
  49.0 36.8 %all-to-all-start.1 = ((bf16[64,2,2048]{2,1,0:T(2,128)(2,1)}), bf16[64,2,2048]{2,1,0:T(2,128)(2,1)S(1)}, u32[]{:S(2)}, u32[]{:S(2)}) async-start(bf16[64,2,2048]{2,1,0:T(2,128)(2,1)} %reshape.87), calls=%async_computation.1 | async-start | bytes 1048576 | tf_op jit(solution)/shard_map/all_to_all | solution.py:81
  58.7 35.9 %copy-start.3 = (bf16[4,1,32,2048]{3,2,1,0:T(8,128)(2,1)S(1)}, bf16[4,1,32,2048]{3,2,1,0:T(8,128)(2,1)}, u32[]{:S(2)}) copy-start(bf16[4,1,32,2048]{3,2,1,0:T(8,128)(2,1)} %param.9) | copy-start | bytes 1572868
  85.8 36.9 %all-to-all-start.2 = ((bf16[64,2,2048]{2,1,0:T(2,128)(2,1)}), bf16[64,2,2048]{2,1,0:T(2,128)(2,1)}, u32[]{:S(2)}, u32[]{:S(2)}) async-start(bf16[64,2,2048]{2,1,0:T(2,128)(2,1)} %reshape.89), calls=%async_computation.2 | async-start | bytes 1048576 | tf_op jit(solution)/shard_map/all_to_all | solution.py:82
  122.8 66.2 %all-to-all-start.5 = ((bf16[4,1,32,2048]{3,0,1,2:T(4,128)(2,1)}), bf16[4,1,32,2048]{3,0,1,2:T(4,128)(2,1)S(1)}, u32[]{:S(2)}, u32[]{:S(2)}) async-start(bf16[4,1,32,2048]{3,0,1,2:T(4,128)(2,1)} %copy.99), calls=%async_computation.5 | async-start | bytes 1048576 | tf_op jit(solution)/shard_map/all_to_all | solution.py:88
  189.0 36.8 %all-to-all-start.3 = ((bf16[64,2,2048]{2,1,0:T(2,128)(2,1)}), bf16[64,2,2048]{2,1,0:T(2,128)(2,1)S(1)}, u32[]{:S(2)}, u32[]{:S(2)}) async-start(bf16[64,2,2048]{2,1,0:T(2,128)(2,1)} %reshape.91), calls=%async_computation.3 | async-start | bytes 1048576 | tf_op jit(solution)/shard_map/all_to_all | solution.py:85
  225.8 49.7 %all-to-all-start.6 = ((bf16[4,1,32,2048]{3,0,1,2:T(4,128)(2,1)}), bf16[4,1,32,2048]{3,0,1,2:T(4,128)(2,1)S(1)}, u32[]{:S(2)}, u32[]{:S(2)}) async-start(bf16[4,1,32,2048]{3,0,1,2:T(4,128)(2,1)} %copy.101), calls=%async_computation.6 | async-start | bytes 1048576 | tf_op jit(solution)/shard_map/all_to_all | solution.py:89
  242.4 43.9 %copy-start.1 = (bf16[4,1,32,2048]{3,2,0,1:T(8,128)(2,1)}, bf16[4,1,32,2048]{3,2,0,1:T(8,128)(2,1)S(1)}, u32[]{:S(2)}) copy-start(bf16[4,1,32,2048]{3,2,0,1:T(8,128)(2,1)S(1)} %reshape.76) | copy-start | bytes 1572868
  275.5 23.9 %all-to-all-start.4 = ((bf16[4,1,32,2048]{3,0,1,2:T(4,128)(2,1)}), bf16[4,1,32,2048]{3,0,1,2:T(4,128)(2,1)S(1)}, u32[]{:S(2)}, u32[]{:S(2)}) async-start(bf16[4,1,32,2048]{3,0,1,2:T(4,128)(2,1)} %copy.97), calls=%async_computation.4 | async-start | bytes 1048576 | tf_op jit(solution)/shard_map/all_to_all | solution.py:90
where the time goes:
time: 336 us; the launch traced here: 335 us
  waiting for transfers between devices  144 us (43%)
  starting transfers between devices  69.8 us (21%)
  matrix products  56.6 us (17%)
  local copies, waits for them, and re-layouts  33.4 us (10%)
  blocking collectives  30.1 us (9%)
    all_to_all x1, waiting for transfers between devices, local(): lax.all_to_all(key_rows, 'view', split_axis=2, concat_axis=1, tiled=True)  31.9 us
    all_to_all x1, blocking collectives, local(): lax.all_to_all(combined, 'view', split_axis=1, concat_axis=2, tiled=True)  30.1 us
    sub x4, matrix products, one_block(): scores = scores - jnp.max(scores, axis=-1, keepdims=True)  27.4 us
    all_to_all x1, waiting for transfers between devices, local(): lax.all_to_all(output_pairs, 'seq', split_axis=0, concat_axis=1, tiled=True)  27 us
    all_to_all x1, waiting for transfers between devices, local(): lax.all_to_all(split_heads(key_rows), 'seq', split_axis=1, concat_axis=0,...  24.8 us
    all_to_all x1, waiting for transfers between devices, local(): lax.all_to_all(split_heads(queries), 'seq', split_axis=1, concat_axis=0,...  24.8 us
    all_to_all x1, waiting for transfers between devices, local(): lax.all_to_all(split_heads(value_rows), 'seq', split_axis=1, concat_axis=...  23 us
    dot_general x4, matrix products, one_block(): jnp.einsum('pqk,kpe->qpe', weights, value_pairs, preferred_element_type=j...  22 us
  transfers between devices with their start and end apart: 7, of which 6 were waited for; matrix products, arithmetic and copies ran while one was open for 24% of the time, Pallas kernels for 0%

commit v1 on v0

v1 whole, which is shorter than its diff:
```python
import jax
import jax.numpy as jnp
from jax import lax
from jax.experimental import pallas as pl
from jax.experimental.pallas import tpu as pltpu
from jax.sharding import PartitionSpec as P

MESH = pl.DeviceIdType.MESH
BF16, F32 = jnp.bfloat16, jnp.float32
BATCH, VIEWS, SEQ_LEN, D = 4, 8, 2048, 2048
TOKENS = 32
PAIR = 128
HALF = 64
GROUPS = D // PAIR
SHARE = SEQ_LEN // VIEWS
SCALE = 0.125 * 1.4426950408889634


def rows(start, size):
    return pl.ds(pl.multiple_of(start, TOKENS), size)


def low_lanes(count):
    return lax.broadcasted_iota(jnp.int32, (count, PAIR), 1) < HALF


def split_queries(block):
    low = low_lanes(block.shape[0])
    scaled = block.astype(F32) * SCALE
    first = scaled.astype(BF16).astype(F32)
    second = pltpu.roll(scaled - first, HALF, 1)
    return jnp.where(low, first, second).astype(BF16), jnp.where(low, second, first).astype(BF16)


def twin_keys(block):
    low = low_lanes(block.shape[0])
    plain = block.astype(F32)
    moved = pltpu.roll(plain, HALF, 1)
    return jnp.where(low, plain, moved).astype(BF16), jnp.where(low, moved, plain).astype(BF16)


def values_and_ones(block):
    low = low_lanes(block.shape[0])
    plain = block.astype(F32)
    return jnp.where(low, plain, 1.0).astype(BF16), jnp.where(low, 1.0, plain).astype(BF16)


def weigh(query, key, value, mask=None):
    scores = lax.dot_general(query, key, (((1,), (1,)), ((), ())), preferred_element_type=F32)
    if mask is not None:
        scores = jnp.where(mask, scores, -1e30)
    scores = scores - jnp.max(scores, axis=1, keepdims=True)
    return jnp.dot(jnp.exp2(scores).astype(BF16), value, preferred_element_type=F32)


def finish(first, second):
    low = low_lanes(first.shape[0])
    total = pltpu.roll(jnp.where(low, second, first), HALF, 1)
    return (jnp.where(low, first, second) / total).astype(BF16)


def kernel(
    queries, key_rows, value_rows, view_queries, spatial, joined,
    k_in, v_in, q_in, w_in, k_a, k_b, v_a, v_b, o_out, k_views, o_views, j_out,
    in_sent, in_here, k_sent, k_here, o_sent, o_here, home_sent, home_here,
):
    view, seq = lax.axis_index("view"), lax.axis_index("seq")
    z_hi, y = view // 4, view % 4
    z_lo, x, core = seq // 8, (seq // 2) % 4, seq % 2
    z = z_hi * 8 + z_lo
    my_pair = z * 4 + x
    my_view = core * 4 + y
    b, g = my_pair // GROUPS, my_pair % GROUPS
    view_stays = z_hi == core
    share_stays = z_lo == my_view

    def at(z, y, x, core):
        return ((z // 8) * 4 + y, (z % 8) * 8 + x * 2 + core)

    def place(ref, b, g):
        return ref.at[b, 0, :, pl.ds(pl.multiple_of(g * PAIR, PAIR), PAIR)]

    def send(src, dst, sent, here, device, stays):
        @pl.when(jnp.logical_not(stays))
        def _():
            pltpu.make_async_remote_copy(src, dst, sent, here, device_id=device, device_id_type=MESH).start()

        @pl.when(stays)
        def _():
            pltpu.make_async_copy(src, dst, here).start()

    def wait(ref, sem):
        pltpu.make_async_copy(ref, ref, sem).wait()

    def wait_sent(sem, stays):
        @pl.when(stays)
        def _():
            wait(q_in.at[pl.ds(0, SEQ_LEN - TOKENS)], sem)

        @pl.when(jnp.logical_not(stays))
        def _():
            wait(q_in, sem)

    barrier = pltpu.get_barrier_semaphore()

    def greet(device, stays):
        @pl.when(jnp.logical_not(stays))
        def _():
            pl.semaphore_signal(barrier, inc=1, device_id=device, device_id_type=MESH)

    @pl.loop(0, 64)
    def _(i):
        c2, x2, z2 = i % 2, (i // 2) % 4, i // 8
        greet(at(core * 8 + z2, y, x2, c2), view_stays & (z2 == z_lo) & (x2 == x) & (c2 == core))
        greet(at((i // 32) * 8 + my_view, (i // 8) % 4, x2, c2), share_stays & (i // 8 == view) & (x2 == x) & (c2 == core))

    @pl.loop(1, VIEWS)
    def _(i):
        other = (my_view + i) % VIEWS
        greet(at(z, other % 4, x, other // 4), False)

    expected = 2 * 64 + VIEWS - 1 - view_stays.astype(jnp.int32) - share_stays.astype(jnp.int32)
    pl.semaphore_wait(barrier, expected)

    for which, (array, buffer) in enumerate(((key_rows, k_in), (value_rows, v_in), (queries, q_in))):

        @pl.loop(0, 64)
        def _(i):
            z2, x2 = (z + i // 4) % 16, (x + i) % 4
            pair = z2 * 4 + x2
            send(
                place(array, pair // GROUPS, pair % GROUPS),
                buffer.at[rows(seq * TOKENS, TOKENS)],
                in_sent.at[which],
                in_here.at[which],
                at(z2, y, x2, z_hi),
                view_stays & (i == 0),
            )

    @pl.loop(0, 64)
    def _(i):
        z2, x2 = (z + i // 4) % 16, (x + i) % 4
        pair = z2 * 4 + x2
        send(
            place(view_queries, pair // GROUPS, pair % GROUPS),
            w_in.at[view, rows((seq % 8) * TOKENS, TOKENS)],
            in_sent.at[3],
            in_here.at[3],
            at(z2, z_lo % 4, x2, z_lo // 4),
            share_stays & (i == 0),
        )

    wait(k_in, in_here.at[0])

    @pl.loop(0, VIEWS)
    def _(i):
        other = (my_view + i) % VIEWS
        send(
            k_in.at[rows(other * SHARE, SHARE)],
            k_views.at[my_view],
            k_sent,
            k_here,
            at(z, other % 4, x, other // 4),
            i == 0,
        )

    k_a[...], k_b[...] = twin_keys(k_in[...])
    wait(v_in, in_here.at[1])
    v_a[...], v_b[...] = values_and_ones(v_in[...])
    wait(q_in, in_here.at[2])

    @pl.loop(0, VIEWS)
    def _(i):
        part = (z_lo + i) % VIEWS
        here = rows(part * SHARE, SHARE)
        q_a, q_b = split_queries(q_in[here])
        o_out[here] = finish(weigh(q_a, k_a[...], v_a[...]), weigh(q_b, k_b[...], v_b[...]))
        send(
            o_out.at[here],
            o_views.at[my_view],
            o_sent,
            o_here,
            at(z, part % 4, x, part // 4),
            part == my_view,
        )

        @pl.loop(0, 8)
        def _(n):
            x2, c2 = (x + n // 2) % 4, n % 2
            send(
                o_out.at[rows(part * SHARE + (x2 * 2 + c2) * TOKENS, TOKENS)],
                place(spatial, b, g),
                home_sent.at[0],
                home_here.at[0],
                at(core * 8 + part, y, x2, c2),
                view_stays & (part == z_lo) & (x2 == x) & (c2 == core),
            )

    wait(k_views, k_here)
    wait(w_in, in_here.at[3])
    wait(o_views, o_here)
    count = VIEWS * TOKENS
    same = (
        lax.broadcasted_iota(jnp.int32, (count, count), 0) % TOKENS
        == lax.broadcasted_iota(jnp.int32, (count, count), 1) % TOKENS
    )

    @pl.loop(0, 8)
    def _(i):
        x2, c2 = (x + i // 2) % 4, i % 2
        here = rows((x2 * 2 + c2) * TOKENS, TOKENS)
        q_1, q_2 = split_queries(w_in[:, here].reshape(count, PAIR))
        k_1, k_2 = twin_keys(k_views[:, here].reshape(count, PAIR))
        v_1, v_2 = values_and_ones(o_views[:, here].reshape(count, PAIR))
        result = finish(weigh(q_1, k_1, v_1, same), weigh(q_2, k_2, v_2, same))
        j_out[:, here] = result.reshape(VIEWS, TOKENS, PAIR)

        @pl.loop(0, VIEWS)
        def _(n):
            v2 = (view + n) % VIEWS
            send(
                j_out.at[v2, here],
                place(joined, b, g),
                home_sent.at[1],
                home_here.at[1],
                at((v2 // 4) * 8 + my_view, v2 % 4, x2, c2),
                share_stays & (n == 0) & (i // 2 == 0) & (c2 == core),
            )

    for which, stays in enumerate((view_stays, view_stays, view_stays, share_stays)):
        wait_sent(in_sent.at[which], stays)
    wait(q_in.at[pl.ds(0, SEQ_LEN - SHARE)], k_sent)
    wait(q_in.at[pl.ds(0, SEQ_LEN - SHARE)], o_sent)
    wait_sent(home_sent.at[0], view_stays)
    wait_sent(home_sent.at[1], share_stays)
    wait(spatial, home_here.at[0])
    wait(joined, home_here.at[1])


def local(queries, key_rows, value_rows, view_queries):
    whole, shares = (SEQ_LEN, PAIR), (VIEWS, SHARE, PAIR)
    return pl.pallas_call(
        kernel,
        out_shape=[jax.ShapeDtypeStruct(queries.shape, BF16)] * 2,
        in_specs=[pl.BlockSpec(memory_space=pl.ANY)] * 4,
        out_specs=[pl.BlockSpec(memory_space=pl.ANY)] * 2,
        scratch_shapes=[
            *[pltpu.VMEM(whole, BF16)] * 3,
            pltpu.VMEM(shares, BF16),
            *[pltpu.VMEM(whole, BF16)] * 5,
            *[pltpu.VMEM(shares, BF16)] * 3,
            pltpu.SemaphoreType.DMA((4,)),
            pltpu.SemaphoreType.DMA((4,)),
            *[pltpu.SemaphoreType.DMA] * 4,
            pltpu.SemaphoreType.DMA((2,)),
            pltpu.SemaphoreType.DMA((2,)),
        ],
        compiler_params=pltpu.CompilerParams(
            collective_id=0, has_side_effects=True, vmem_limit_bytes=48 << 20
        ),
        cost_estimate=pl.CostEstimate(flops=1 << 32, bytes_accessed=1 << 22, transcendentals=1 << 23),
    )(queries, key_rows, value_rows, view_queries)


def solution(mesh):
    placed = P(None, "view", "seq", None)
    return jax.shard_map(
        local, mesh=mesh, in_specs=(placed,) * 4, out_specs=(placed, placed), check_vma=False
    )
```

time: 336 us -> 178 us (0.53)
  the two profiles are of different devices: /device:TPU:32 before, /device:TPU:1 now
where the time goes in v1:
time: 178 us; the launch traced here: 176 us
  Pallas kernels  169 us (95%)
  local copies, waits for them, and re-layouts  5.75 us (3%)
    pallas_call x1, Pallas kernels, local(): pl.pallas_call(kernel, out_shape=[jax.ShapeDtypeStruct(queries.shape, BF1...  169 us
    unnamed x10, local copies, waits for them, and re-layouts  5.75 us

profile of v1, /device:TPU:1, one launch (start us, length us, event | category | flops | bytes accessed | tf_op | source)
XLA Modules:
  0.0 175.7 jit_solution(14647557706169742091)
XLA Ops:
  0.6 0.0 copy-start
  0.6 1.0 copy-done
  1.7 0.0 copy-start.1
  1.7 1.0 copy-done.1
  2.7 0.0 copy-start.2
  2.7 1.0 copy-done.2
  3.8 0.0 copy-start.3
  3.8 1.0 copy-done.3
  4.8 169.3 %shard_map.59 = (bf16[4,1,32,2048]{3,2,1,0:T(8,128)(2,1)S(1)}, bf16[4,1,32,2048]{3,2,1,0:T(8,128)(2,1)S(1)}) custom-call(bf16[4,1,32,2048]{3,2,1,0:T(8,128)(2,1)S(1)} %copy-done, bf16[4,1,32,2048]{3,2,1,0:T(8,128)(2,1)S(1)} %copy-done.1, bf16[4,1,32,2048]{3,2,1,0:T(8,128)(2,1)S(1)} %copy-done.2, bf16[4,1,32,2048]{3,2,1,0:T(8,128)(2,1)S(1)} %copy-done.3), custom_call_target="tpu_custom_call" | custom-call | flops 4294967296 | bytes 4194304 | tf_op jit(solution)/shard_map/pallas_call | solution.py:242
  174.1 0.8 copy.8
  174.9 0.8 copy.9
Async XLA Ops:
  0.6 1.0 copy-start
  1.7 1.0 copy-start.1
  2.7 1.0 copy-start.2
  3.8 1.0 copy-start.3

commit v2 on v1

--- a/solution.py
+++ b/solution.py
@@ -62,7 +62,7 @@
 def kernel(
     queries, key_rows, value_rows, view_queries, spatial, joined,
     k_in, v_in, q_in, w_in, k_a, k_b, v_a, v_b, o_out, k_views, o_views, j_out,
-    in_sent, in_here, k_sent, k_here, o_sent, o_here, home_sent, home_here,
+    in_sent, in_here, q_here, leave, k_sent, k_here, o_sent, o_here, home_sent, home_here,
 ):
     view, seq = lax.axis_index("view"), lax.axis_index("seq")
     z_hi, y = view // 4, view % 4
@@ -72,11 +72,20 @@
     my_view = core * 4 + y
     b, g = my_pair // GROUPS, my_pair % GROUPS
     view_stays = z_hi == core
-    share_stays = z_lo == my_view
+    my_share = (y % 2) + 2 * core + 4 * (y // 2)
+    turn = z_lo + x + 4 * core
+    share_stays = (turn + x) % VIEWS == my_share
 
     def at(z, y, x, core):
         return ((z // 8) * 4 + y, (z % 8) * 8 + x * 2 + core)
 
+    def combiner(share):
+        return (share % 2) + 2 * (share // 4), (share // 2) % 2
+
+    def home_of(share, part):
+        turn = (share - x - part + 2 * VIEWS) % VIEWS
+        return turn % 4, turn // 4
+
     def place(ref, b, g):
         return ref.at[b, 0, :, pl.ds(pl.multiple_of(g * PAIR, PAIR), PAIR)]
 
@@ -102,90 +111,87 @@
             wait(q_in, sem)
 
     barrier = pltpu.get_barrier_semaphore()
-
-    def greet(device, stays):
-        @pl.when(jnp.logical_not(stays))
-        def _():
-            pl.semaphore_signal(barrier, inc=1, device_id=device, device_id_type=MESH)
-
-    @pl.loop(0, 64)
-    def _(i):
-        c2, x2, z2 = i % 2, (i // 2) % 4, i // 8
-        greet(at(core * 8 + z2, y, x2, c2), view_stays & (z2 == z_lo) & (x2 == x) & (c2 == core))
-        greet(at((i // 32) * 8 + my_view, (i // 8) % 4, x2, c2), share_stays & (i // 8 == view) & (x2 == x) & (c2 == core))
-
-    @pl.loop(1, VIEWS)
-    def _(i):
+    first = view_stays.astype(jnp.int32)
+
+    @pl.loop(first, 64)
+    def _(i):
+        pl.semaphore_signal(barrier, inc=1, device_id=(my_view, (seq + i) % 64), device_id_type=MESH)
+
+    for i in range(1, VIEWS):
         other = (my_view + i) % VIEWS
-        greet(at(z, other % 4, x, other // 4), False)
-
-    expected = 2 * 64 + VIEWS - 1 - view_stays.astype(jnp.int32) - share_stays.astype(jnp.int32)
-    pl.semaphore_wait(barrier, expected)
+        pl.semaphore_signal(barrier, inc=1, device_id=at(z, other % 4, x, other // 4), device_id_type=MESH)
+    pl.semaphore_wait(barrier, 64 + VIEWS - 1 - first)
+
+    def scatter(array, step, target):
+        for dx in range(4):
+            z2, x2 = (z + step) % 16, (x + dx) % 4
+            pair = z2 * 4 + x2
+            target(place(array, pair // GROUPS, pair % GROUPS), z2, x2, (step == 0) & (dx == 0))
 
     for which, (array, buffer) in enumerate(((key_rows, k_in), (value_rows, v_in), (queries, q_in))):
 
-        @pl.loop(0, 64)
-        def _(i):
-            z2, x2 = (z + i // 4) % 16, (x + i) % 4
-            pair = z2 * 4 + x2
-            send(
-                place(array, pair // GROUPS, pair % GROUPS),
-                buffer.at[rows(seq * TOKENS, TOKENS)],
-                in_sent.at[which],
-                in_here.at[which],
-                at(z2, y, x2, z_hi),
-                view_stays & (i == 0),
-            )
-
-    @pl.loop(0, 64)
-    def _(i):
-        z2, x2 = (z + i // 4) % 16, (x + i) % 4
-        pair = z2 * 4 + x2
-        send(
-            place(view_queries, pair // GROUPS, pair % GROUPS),
-            w_in.at[view, rows((seq % 8) * TOKENS, TOKENS)],
-            in_sent.at[3],
-            in_here.at[3],
-            at(z2, z_lo % 4, x2, z_lo // 4),
-            share_stays & (i == 0),
-        )
+        @pl.loop(0, 16)
+        def _(step):
+            def target(src, z2, x2, own):
+                if which == 2:
+                    row = seq * TOKENS
+                else:
+                    row = (turn + x2) % VIEWS * SHARE + z_lo * TOKENS
+                dst = buffer.at[rows(row, TOKENS)]
+                here = q_here.at[z_lo] if which == 2 else in_here.at[which]
+                send(src, dst, in_sent.at[which], here, at(z2, y, x2, z_hi), view_stays & own)
+
+            scatter(array, step, target)
 
     wait(k_in, in_here.at[0])
 
-    @pl.loop(0, VIEWS)
-    def _(i):
-        other = (my_view + i) % VIEWS
-        send(
-            k_in.at[rows(other * SHARE, SHARE)],
-            k_views.at[my_view],
-            k_sent,
-            k_here,
-            at(z, other % 4, x, other // 4),
-            i == 0,
-        )
+    @pl.loop(first, 64)
+    def _(i):
+        pl.semaphore_signal(leave, inc=1, device_id=(my_view, (seq + i) % 64), device_id_type=MESH)
+
+    @pl.loop(0, VIEWS)
+    def _(i):
+        share = (my_share + i) % VIEWS
+        y2, c2 = combiner(share)
+        send(k_in.at[rows(share * SHARE, SHARE)], k_views.at[my_view], k_sent, k_here, at(z, y2, x, c2), i == 0)
 
     k_a[...], k_b[...] = twin_keys(k_in[...])
+    pl.semaphore_wait(leave, 64 - first)
     wait(v_in, in_here.at[1])
     v_a[...], v_b[...] = values_and_ones(v_in[...])
-    wait(q_in, in_here.at[2])
-
-    @pl.loop(0, VIEWS)
-    def _(i):
-        part = (z_lo + i) % VIEWS
+
+    @pl.loop(0, VIEWS)
+    def _(i):
+        part = (jnp.where(view_stays, z_lo, 7) + VIEWS - i) % VIEWS
         here = rows(part * SHARE, SHARE)
+        wait(q_in.at[here], q_here.at[part])
         q_a, q_b = split_queries(q_in[here])
         o_out[here] = finish(weigh(q_a, k_a[...], v_a[...]), weigh(q_b, k_b[...], v_b[...]))
-        send(
-            o_out.at[here],
-            o_views.at[my_view],
-            o_sent,
-            o_here,
-            at(z, part % 4, x, part // 4),
-            part == my_view,
-        )
-
-        @pl.loop(0, 8)
-        def _(n):
+        for n in range(8):
+            share = (my_share + n) % VIEWS
+            y2, c2 = combiner(share)
+            x2, from2 = home_of(share, part)
+            send(
+                o_out.at[rows(part * SHARE + (x2 * 2 + from2) * TOKENS, TOKENS)],
+                o_views.at[my_view, rows(part * TOKENS, TOKENS)],
+                o_sent,
+                o_here,
+                at(z, y2, x, c2),
+                n == 0,
+            )
+
+        def target(src, z2, x2, own):
+            y2, c2 = combiner((turn + x2) % VIEWS)
+            dst = w_in.at[view, rows(z_lo * TOKENS, TOKENS)]
+            send(src, dst, in_sent.at[3], in_here.at[3], at(z2, y2, x2, c2), share_stays & own)
+
+        scatter(view_queries, 2 * i, target)
+        scatter(view_queries, 2 * i + 1, target)
+
+    @pl.loop(0, VIEWS)
+    def _(i):
+        part = (jnp.where(view_stays, z_lo, 7) + VIEWS - i) % VIEWS
+        for n in range(8):
             x2, c2 = (x + n // 2) % 4, n % 2
             send(
                 o_out.at[rows(part * SHARE + (x2 * 2 + c2) * TOKENS, TOKENS)],
@@ -205,26 +211,26 @@
         == lax.broadcasted_iota(jnp.int32, (count, count), 1) % TOKENS
     )
 
-    @pl.loop(0, 8)
-    def _(i):
-        x2, c2 = (x + i // 2) % 4, i % 2
-        here = rows((x2 * 2 + c2) * TOKENS, TOKENS)
+    @pl.loop(0, VIEWS)
+    def _(i):
+        part = (z_lo + i) % VIEWS
+        x2, c2 = home_of(my_share, part)
+        here = rows(part * TOKENS, TOKENS)
         q_1, q_2 = split_queries(w_in[:, here].reshape(count, PAIR))
         k_1, k_2 = twin_keys(k_views[:, here].reshape(count, PAIR))
         v_1, v_2 = values_and_ones(o_views[:, here].reshape(count, PAIR))
         result = finish(weigh(q_1, k_1, v_1, same), weigh(q_2, k_2, v_2, same))
         j_out[:, here] = result.reshape(VIEWS, TOKENS, PAIR)
 
-        @pl.loop(0, VIEWS)
-        def _(n):
+        for n in range(VIEWS):
             v2 = (view + n) % VIEWS
             send(
                 j_out.at[v2, here],
                 place(joined, b, g),
                 home_sent.at[1],
                 home_here.at[1],
-                at((v2 // 4) * 8 + my_view, v2 % 4, x2, c2),
-                share_stays & (n == 0) & (i // 2 == 0) & (c2 == core),
+                at((v2 // 4) * 8 + part, v2 % 4, x2, c2),
+                share_stays & (n == 0) & (i == 0),
             )
 
     for which, stays in enumerate((view_stays, view_stays, view_stays, share_stays)):
@@ -251,12 +257,14 @@
             *[pltpu.VMEM(shares, BF16)] * 3,
             pltpu.SemaphoreType.DMA((4,)),
             pltpu.SemaphoreType.DMA((4,)),
+            pltpu.SemaphoreType.DMA((VIEWS,)),
+            pltpu.SemaphoreType.REGULAR,
             *[pltpu.SemaphoreType.DMA] * 4,
             pltpu.SemaphoreType.DMA((2,)),
             pltpu.SemaphoreType.DMA((2,)),
         ],
         compiler_params=pltpu.CompilerParams(
-            collective_id=0, has_side_effects=True, vmem_limit_bytes=48 << 20
+            collective_id=0, has_side_effects=True, vmem_limit_bytes=60 << 20
         ),
         cost_estimate=pl.CostEstimate(flops=1 << 32, bytes_accessed=1 << 22, transcendentals=1 << 23),
     )(queries, key_rows, value_rows, view_queries)

time: 178 us -> 164 us (0.921); the launches traced: 176 us -> 164 us
  Pallas kernels: 169 us -> 161 us
  local copies, waits for them, and re-layouts: 5.75 us -> 2.74 us
    pallas_call x1, Pallas kernels: 169 us -> 161 us  [local(): pl.pallas_call(kernel, out_shape=[jax.ShapeDtypeStruct(queries.shape, BF1...]
    unnamed x10 -> x4, local copies, waits for them, and re-layouts: 5.75 us -> 2.74 us
where the time goes in v2:
time: 164 us
  Pallas kernels  161 us (98%)
  local copies, waits for them, and re-layouts  2.74 us (2%)
    pallas_call x1, Pallas kernels, local(): pl.pallas_call(kernel, out_shape=[jax.ShapeDtypeStruct(queries.shape, BF1...  161 us

profile of v2, /device:TPU:1, one launch (start us, length us, event | category | flops | bytes accessed | tf_op | source)
XLA Modules:
  0.0 164.2 jit_solution(7176921089488263764)
XLA Ops:
  0.6 160.8 %shard_map.59 = (bf16[4,1,32,2048]{3,2,1,0:T(8,128)(2,1)}, bf16[4,1,32,2048]{3,2,1,0:T(8,128)(2,1)}) custom-call(bf16[4,1,32,2048]{3,2,1,0:T(8,128)(2,1)} %queries.1, bf16[4,1,32,2048]{3,2,1,0:T(8,128)(2,1)} %key_rows.1, bf16[4,1,32,2048]{3,2,1,0:T(8,128)(2,1)} %value_rows.1, bf16[4,1,32,2048]{3,2,1,0:T(8,128)(2,1)} %view_queries.1), custom_call_target="tpu_custom_call" | custom-call | flops 4294967296 | bytes 4194304 | tf_op jit(solution)/shard_map/pallas_call | solution.py:248
  161.5 0.0 copy-start
  161.5 1.9 %copy.8 = bf16[4,1,32,2048]{3,2,1,0:T(8,128)(2,1)} copy(bf16[4,1,32,2048]{3,2,1,0:T(8,128)(2,1)} %get-tuple-element.4) | data formatting | bytes 1048576
  163.4 0.0 copy-done
  163.4 0.8 copy.9
Async XLA Ops:
  161.5 2.0 %copy-start = (bf16[4,1,32,2048]{3,2,1,0:T(8,128)(2,1)S(1)}, bf16[4,1,32,2048]{3,2,1,0:T(8,128)(2,1)}, u32[]{:S(2)}) copy-start(bf16[4,1,32,2048]{3,2,1,0:T(8,128)(2,1)} %get-tuple-element.5) | copy-start | bytes 1572868

commit v3 on v2

--- a/solution.py
+++ b/solution.py
@@ -90,6 +90,14 @@
         return ref.at[b, 0, :, pl.ds(pl.multiple_of(g * PAIR, PAIR), PAIR)]
 
     def send(src, dst, sent, here, device, stays):
+        if stays is False:
+            pltpu.make_async_remote_copy(src, dst, sent, here, device_id=device, device_id_type=MESH).start()
+            return
+
+        if stays is True:
+            pltpu.make_async_copy(src, dst, here).start()
+            return
+
         @pl.when(jnp.logical_not(stays))
         def _():
             pltpu.make_async_remote_copy(src, dst, sent, here, device_id=device, device_id_type=MESH).start()
@@ -113,9 +121,16 @@
     barrier = pltpu.get_barrier_semaphore()
     first = view_stays.astype(jnp.int32)
 
-    @pl.loop(first, 64)
-    def _(i):
-        pl.semaphore_signal(barrier, inc=1, device_id=(my_view, (seq + i) % 64), device_id_type=MESH)
+    def tell_tokens(sem):
+        @pl.when(jnp.logical_not(view_stays))
+        def _():
+            pl.semaphore_signal(sem, inc=1, device_id=(my_view, seq), device_id_type=MESH)
+
+        @pl.loop(1, 64, unroll=9)
+        def _(i):
+            pl.semaphore_signal(sem, inc=1, device_id=(my_view, lax.rem(seq + i, 64)), device_id_type=MESH)
+
+    tell_tokens(barrier)
 
     for i in range(1, VIEWS):
         other = (my_view + i) % VIEWS
@@ -123,14 +138,17 @@
     pl.semaphore_wait(barrier, 64 + VIEWS - 1 - first)
 
     def scatter(array, step, target):
-        for dx in range(4):
-            z2, x2 = (z + step) % 16, (x + dx) % 4
-            pair = z2 * 4 + x2
-            target(place(array, pair // GROUPS, pair % GROUPS), z2, x2, (step == 0) & (dx == 0))
+        for far in (0, 8):
+            z2 = (z + step + far) % 16
+            for dx in range(4):
+                x2 = (x + dx) % 4
+                pair = z2 * 4 + x2
+                own = step == 0 if (far, dx) == (0, 0) else False
+                target(place(array, pair // GROUPS, pair % GROUPS), z2, x2, own)
 
     for which, (array, buffer) in enumerate(((key_rows, k_in), (value_rows, v_in), (queries, q_in))):
 
-        @pl.loop(0, 16)
+        @pl.loop(0, 8)
         def _(step):
             def target(src, z2, x2, own):
                 if which == 2:
@@ -139,15 +157,13 @@
                     row = (turn + x2) % VIEWS * SHARE + z_lo * TOKENS
                 dst = buffer.at[rows(row, TOKENS)]
                 here = q_here.at[z_lo] if which == 2 else in_here.at[which]
-                send(src, dst, in_sent.at[which], here, at(z2, y, x2, z_hi), view_stays & own)
+                send(src, dst, in_sent.at[which], here, at(z2, y, x2, z_hi), False if own is False else view_stays & own)
 
             scatter(array, step, target)
 
     wait(k_in, in_here.at[0])
 
-    @pl.loop(first, 64)
-    def _(i):
-        pl.semaphore_signal(leave, inc=1, device_id=(my_view, (seq + i) % 64), device_id_type=MESH)
+    tell_tokens(leave)
 
     @pl.loop(0, VIEWS)
     def _(i):
@@ -157,12 +173,22 @@
 
     k_a[...], k_b[...] = twin_keys(k_in[...])
     pl.semaphore_wait(leave, 64 - first)
+
+    @pl.loop(0, VIEWS)
+    def _(i):
+        def target(src, z2, x2, own):
+            y2, c2 = combiner((turn + x2) % VIEWS)
+            dst = w_in.at[view, rows(z_lo * TOKENS, TOKENS)]
+            send(src, dst, in_sent.at[3], in_here.at[3], at(z2, y2, x2, c2), False if own is False else share_stays & own)
+
+        scatter(view_queries, i, target)
+
     wait(v_in, in_here.at[1])
     v_a[...], v_b[...] = values_and_ones(v_in[...])
 
     @pl.loop(0, VIEWS)
     def _(i):
-        part = (jnp.where(view_stays, z_lo, 7) + VIEWS - i) % VIEWS
+        part = (z_lo + VIEWS - i) % VIEWS
         here = rows(part * SHARE, SHARE)
         wait(q_in.at[here], q_here.at[part])
         q_a, q_b = split_queries(q_in[here])
@@ -180,26 +206,19 @@
                 n == 0,
             )
 
-        def target(src, z2, x2, own):
-            y2, c2 = combiner((turn + x2) % VIEWS)
-            dst = w_in.at[view, rows(z_lo * TOKENS, TOKENS)]
-            send(src, dst, in_sent.at[3], in_here.at[3], at(z2, y2, x2, c2), share_stays & own)
-
-        scatter(view_queries, 2 * i, target)
-        scatter(view_queries, 2 * i + 1, target)
-
-    @pl.loop(0, VIEWS)
-    def _(i):
-        part = (jnp.where(view_stays, z_lo, 7) + VIEWS - i) % VIEWS
+
+    @pl.loop(0, VIEWS)
+    def _(i):
+        part = (z_lo + VIEWS - i) % VIEWS
         for n in range(8):
-            x2, c2 = (x + n // 2) % 4, n % 2
+            x2, c2 = (x + n // 2) % 4, (core + n) % 2
             send(
                 o_out.at[rows(part * SHARE + (x2 * 2 + c2) * TOKENS, TOKENS)],
                 place(spatial, b, g),
                 home_sent.at[0],
                 home_here.at[0],
                 at(core * 8 + part, y, x2, c2),
-                view_stays & (part == z_lo) & (x2 == x) & (c2 == core),
+                view_stays & (i == 0) if n == 0 else False,
             )
 
     wait(k_views, k_here)
@@ -213,7 +232,7 @@
 
     @pl.loop(0, VIEWS)
     def _(i):
-        part = (z_lo + i) % VIEWS
+        part = (z_lo + VIEWS - i) % VIEWS
         x2, c2 = home_of(my_share, part)
         here = rows(part * TOKENS, TOKENS)
         q_1, q_2 = split_queries(w_in[:, here].reshape(count, PAIR))
@@ -230,7 +249,7 @@
                 home_sent.at[1],
                 home_here.at[1],
                 at((v2 // 4) * 8 + part, v2 % 4, x2, c2),
-                share_stays & (n == 0) & (i == 0),
+                share_stays & (i == 0) if n == 0 else False,
             )
 
     for which, stays in enumerate((view_stays, view_stays, view_stays, share_stays)):
@@ -264,7 +283,7 @@
             pltpu.SemaphoreType.DMA((2,)),
         ],
         compiler_params=pltpu.CompilerParams(
-            collective_id=0, has_side_effects=True, vmem_limit_bytes=60 << 20
+            collective_id=0, has_side_effects=True, vmem_limit_bytes=105 << 19
         ),
         cost_estimate=pl.CostEstimate(flops=1 << 32, bytes_accessed=1 << 22, transcendentals=1 << 23),
     )(queries, key_rows, value_rows, view_queries)

time: 164 us -> 161 us (0.982)
  Pallas kernels: 161 us -> 159 us
    pallas_call x1, Pallas kernels: 161 us -> 159 us  [local(): pl.pallas_call(kernel, out_shape=[jax.ShapeDtypeStruct(queries.shape, BF1...]
where the time goes in v3:
time: 161 us
  Pallas kernels  159 us (99%)
    pallas_call x1, Pallas kernels, local(): pl.pallas_call(kernel, out_shape=[jax.ShapeDtypeStruct(queries.shape, BF1...  159 us

profile of v3, /device:TPU:1, one launch (start us, length us, event | category | flops | bytes accessed | tf_op | source)
XLA Modules:
  0.0 161.1 jit_solution(16245605795344355725)
XLA Ops:
  0.6 158.9 %shard_map.59 = (bf16[4,1,32,2048]{3,2,1,0:T(8,128)(2,1)S(1)}, bf16[4,1,32,2048]{3,2,1,0:T(8,128)(2,1)S(1)}) custom-call(bf16[4,1,32,2048]{3,2,1,0:T(8,128)(2,1)} %queries.1, bf16[4,1,32,2048]{3,2,1,0:T(8,128)(2,1)} %key_rows.1, bf16[4,1,32,2048]{3,2,1,0:T(8,128)(2,1)} %value_rows.1, bf16[4,1,32,2048]{3,2,1,0:T(8,128)(2,1)} %view_queries.1), custom_call_target="tpu_custom_call" | custom-call | flops 4294967296 | bytes 4194304 | tf_op jit(solution)/shard_map/pallas_call | solution.py:267
  159.5 0.8 copy.8
  160.3 0.8 copy.9

commit v4 on v3

--- a/solution.py
+++ b/solution.py
@@ -13,6 +13,7 @@
 HALF = 64
 GROUPS = D // PAIR
 SHARE = SEQ_LEN // VIEWS
+LATER = 6
 SCALE = 0.125 * 1.4426950408889634
 
 
@@ -230,10 +231,23 @@
         == lax.broadcasted_iota(jnp.int32, (count, count), 1) % TOKENS
     )
 
-    @pl.loop(0, VIEWS)
-    def _(i):
-        part = (z_lo + VIEWS - i) % VIEWS
+    def send_joined(i, high):
+        part = (i // 4) * 4 + (z_lo + VIEWS - i) % 4
         x2, c2 = home_of(my_share, part)
+        for n in range(4):
+            y2 = (y + n) % 4
+            send(
+                j_out.at[4 * high + y2, rows(part * TOKENS, TOKENS)],
+                place(joined, b, g),
+                home_sent.at[1],
+                home_here.at[1],
+                at(high * 8 + part, y2, x2, c2),
+                share_stays & (part == z_lo) & (z_hi == high) if n == 0 else False,
+            )
+
+    @pl.loop(0, VIEWS)
+    def _(i):
+        part = (i // 4) * 4 + (z_lo + VIEWS - i) % 4
         here = rows(part * TOKENS, TOKENS)
         q_1, q_2 = split_queries(w_in[:, here].reshape(count, PAIR))
         k_1, k_2 = twin_keys(k_views[:, here].reshape(count, PAIR))
@@ -241,16 +255,15 @@
         result = finish(weigh(q_1, k_1, v_1, same), weigh(q_2, k_2, v_2, same))
         j_out[:, here] = result.reshape(VIEWS, TOKENS, PAIR)
 
-        for n in range(VIEWS):
-            v2 = (view + n) % VIEWS
-            send(
-                j_out.at[v2, here],
-                place(joined, b, g),
-                home_sent.at[1],
-                home_here.at[1],
-                at((v2 // 4) * 8 + part, v2 % 4, x2, c2),
-                share_stays & (i == 0) if n == 0 else False,
-            )
+        send_joined(i, 0)
+
+        @pl.when(i >= LATER)
+        def _():
+            send_joined(i - LATER, 1)
+
+    @pl.loop(VIEWS - LATER, VIEWS)
+    def _(i):
+        send_joined(i, 1)
 
     for which, stays in enumerate((view_stays, view_stays, view_stays, share_stays)):
         wait_sent(in_sent.at[which], stays)

time: 161 us -> 158 us (0.981)
  Pallas kernels: 159 us -> 155 us
    pallas_call x1, Pallas kernels: 159 us -> 155 us  [local(): pl.pallas_call(kernel, out_shape=[jax.ShapeDtypeStruct(queries.shape, BF1...]
where the time goes in v4:
time: 158 us; the launch traced here: 157 us
  Pallas kernels  155 us (98%)
  local copies, waits for them, and re-layouts  1.59 us (1%)
    pallas_call x1, Pallas kernels, local(): pl.pallas_call(kernel, out_shape=[jax.ShapeDtypeStruct(queries.shape, BF1...  155 us

profile of v4, /device:TPU:1, one launch (start us, length us, event | category | flops | bytes accessed | tf_op | source)
XLA Modules:
  0.0 156.9 jit_solution(16474157029424582170)
XLA Ops:
  0.6 154.6 %shard_map.59 = (bf16[4,1,32,2048]{3,2,1,0:T(8,128)(2,1)S(1)}, bf16[4,1,32,2048]{3,2,1,0:T(8,128)(2,1)S(1)}) custom-call(bf16[4,1,32,2048]{3,2,1,0:T(8,128)(2,1)} %queries.1, bf16[4,1,32,2048]{3,2,1,0:T(8,128)(2,1)} %key_rows.1, bf16[4,1,32,2048]{3,2,1,0:T(8,128)(2,1)} %value_rows.1, bf16[4,1,32,2048]{3,2,1,0:T(8,128)(2,1)} %view_queries.1), custom_call_target="tpu_custom_call" | custom-call | flops 4294967296 | bytes 4194304 | tf_op jit(solution)/shard_map/pallas_call | solution.py:280
  155.3 0.8 copy.8
  156.1 0.8 copy.9

commit v5 on v4

--- a/solution.py
+++ b/solution.py
@@ -232,7 +232,7 @@
     )
 
     def send_joined(i, high):
-        part = (i // 4) * 4 + (z_lo + VIEWS - i) % 4
+        part = (i // 2) * 2 + (z_lo + VIEWS - i) % 2
         x2, c2 = home_of(my_share, part)
         for n in range(4):
             y2 = (y + n) % 4
@@ -247,7 +247,7 @@
 
     @pl.loop(0, VIEWS)
     def _(i):
-        part = (i // 4) * 4 + (z_lo + VIEWS - i) % 4
+        part = (i // 2) * 2 + (z_lo + VIEWS - i) % 2
         here = rows(part * TOKENS, TOKENS)
         q_1, q_2 = split_queries(w_in[:, here].reshape(count, PAIR))
         k_1, k_2 = twin_keys(k_views[:, here].reshape(count, PAIR))

time: 158 us -> 157 us (level)
  no operation moved by 1% of the time
where the time goes in v5:
time: 157 us; the launch traced here: 156 us
  Pallas kernels  154 us (98%)
  local copies, waits for them, and re-layouts  1.59 us (1%)
    pallas_call x1, Pallas kernels, local(): pl.pallas_call(kernel, out_shape=[jax.ShapeDtypeStruct(queries.shape, BF1...  154 us

profile of v5, /device:TPU:1, one launch (start us, length us, event | category | flops | bytes accessed | tf_op | source)
XLA Modules:
  0.0 156.4 jit_solution(5209441994029334925)
XLA Ops:
  0.6 154.2 %shard_map.59 = (bf16[4,1,32,2048]{3,2,1,0:T(8,128)(2,1)S(1)}, bf16[4,1,32,2048]{3,2,1,0:T(8,128)(2,1)S(1)}) custom-call(bf16[4,1,32,2048]{3,2,1,0:T(8,128)(2,1)} %queries.1, bf16[4,1,32,2048]{3,2,1,0:T(8,128)(2,1)} %key_rows.1, bf16[4,1,32,2048]{3,2,1,0:T(8,128)(2,1)} %value_rows.1, bf16[4,1,32,2048]{3,2,1,0:T(8,128)(2,1)} %view_queries.1), custom_call_target="tpu_custom_call" | custom-call | flops 4294967296 | bytes 4194304 | tf_op jit(solution)/shard_map/pallas_call | solution.py:280
  154.8 0.8 copy.8
  155.6 0.8 copy.9
